TPU v7x, 256 devices: a whole 4x4x8 slice. The times are simulated.
256 devices in a mesh: pop: 32 (over y_lo, z, core), fsdp: 8 (over y_hi, x).
Axes of the slice: x: 4, y: 4 (y_hi: 2, y_lo: 2; y = y_hi * 2 + y_lo), z: 8, core: 2. Of those that a mesh axis runs over, the one named last changes fastest.
Arguments:
- tokens: bfloat16 [28672, 4096], P('pop', 'fsdp'), may hold values from -6 to 6
- up_weight: bfloat16 [4096, 14336], P('pop', 'fsdp'), may hold values from -0.09375 to 0.09375
- a_bank: bfloat16 [1024, 4096], P(None, 'pop'), may hold values from -6 to 6
- b_bank: bfloat16 [1024, 14336], P(None, 'fsdp'), may hold values from -6 to 6
- factor_index: int32 [64, 4], replicated, may hold values from 0 to 1023
- mirror: int32 [64], P('pop'), may hold values 0 or 1
- rewards: int32 [64], P('pop'), may hold values from -8 to 7
Outputs:
- hidden: bfloat16 [28672, 14336], P('pop', 'fsdp')
- update: float32 [4096, 14336], P('pop', 'fsdp')
All inputs are finite; a program needn't handle non-finite values. No bound on the sum of `mirror` on one device may be relied on, other than what follows from the above.
Results may differ from a plain program's by a relative error of at most 0.001.
Values may be sent and summed in bfloat16 or wider, within the bound.
A program may use at most 128 MiB of HBM per device.

v0:
```python
import math
import jax
import jax.numpy as jnp
from jax import lax
from jax.sharding import PartitionSpec as P

D = 4096
RANK = 4
SEQ = 448
noise_scale = 0.5


def sent_to_all(array, axis):
    copies = jnp.broadcast_to(array, (lax.axis_size(axis), *array.shape))
    return lax.all_to_all(copies, axis, split_axis=0, concat_axis=0, tiled=True)


def joined_along(parts, dim):
    parts = jnp.moveaxis(parts, 0, dim)
    dims = parts.shape
    return parts.reshape(*dims[:dim], dims[dim] * dims[dim + 1], *dims[dim + 2 :])


def gather_directly(array, axis, dim):
    parts = sent_to_all(array, axis)
    return joined_along(parts, dim)


def shaped_weights(rewards, mirror):
    members_all = rewards.shape[0]
    member_ids = jnp.arange(members_all)
    beaten = rewards[None, :] < rewards[:, None]
    level_tie = (rewards[None, :] == rewards[:, None]) & (member_ids[None, :] < member_ids[:, None])
    standing = jnp.sum((beaten | level_tie).astype(jnp.int32), axis=1)
    signed = (2 * mirror - 1).astype(jnp.float32)
    shaped = 2.0 * standing.astype(jnp.float32) / (members_all - 1) - 1.0
    return shaped * signed / math.sqrt(members_all * RANK)


def per_device(tokens, up_weight, a_bank, b_bank, factor_index, mirror, rewards):
    members_here = mirror.shape[0]
    own_width = members_here * RANK
    position = lax.axis_index("pop")
    flat_index = factor_index.reshape(-1)
    picked_a = jnp.take(a_bank, flat_index, axis=0)
    picked_b = jnp.take(b_bank, flat_index, axis=0)
    first_own = position * own_width
    gathered_a, rewards_all, mirror_all = (
        gather_directly(picked_a, "pop", 1),
        gather_directly(rewards, "pop", 0),
        gather_directly(mirror, "pop", 0),
    )
    own_a = lax.dynamic_slice_in_dim(gathered_a, first_own, own_width, 0)
    own_b = lax.dynamic_slice_in_dim(picked_b, first_own, own_width, 0).astype(jnp.float32)
    own_signs = (2 * mirror - 1).astype(jnp.float32)
    column_factor = jnp.repeat(noise_scale / math.sqrt(D * RANK) * own_signs, RANK)
    member_of_column = jnp.arange(own_width) // RANK
    row_count = tokens.shape[0]
    entire_weight = lax.all_gather(up_weight, "pop", axis=0, tiled=True)
    piece = lax.all_gather(tokens, "fsdp", axis=1, tiled=True)
    dense_sum = jnp.dot(piece, entire_weight, preferred_element_type=jnp.float32)
    low_sum = jnp.dot(piece, own_a.T, preferred_element_type=jnp.float32)
    member_of_row = jnp.arange(row_count) // SEQ
    same_member = member_of_row[:, None] == member_of_column[None, :]
    scaled = jnp.where(same_member, low_sum * column_factor[None, :], 0.0)
    perturbed = jnp.dot(scaled, own_b, precision=lax.Precision.HIGHEST)
    hidden = (dense_sum + perturbed).astype(jnp.bfloat16)
    weighting = shaped_weights(rewards_all, mirror_all)
    spread = jnp.repeat(weighting, RANK)
    update = jnp.dot(
        picked_a.astype(jnp.float32).T,
        spread[:, None] * picked_b.astype(jnp.float32),
        precision=lax.Precision.HIGHEST,
    )
    return (hidden, update)


def solution(mesh):
    in_specs = (
        P("pop", "fsdp"),
        P("pop", "fsdp"),
        P(None, "pop"),
        P(None, "fsdp"),
        P(),
        P("pop"),
        P("pop"),
    )
    out_specs = (P("pop", "fsdp"), P("pop", "fsdp"))
    return jax.shard_map(
        per_device, mesh=mesh, in_specs=in_specs, out_specs=out_specs, check_vma=False
    )
```

profile of v0, /device:TPU:1, one launch (start us, length us, event | category | flops | bytes accessed | tf_op | source)
XLA Modules:
  0.0 262.1 jit_solution(9321200983050298536)
XLA Ops:
  7.2 0.7 all-gather.3.cloned.1.call-update
  8.0 0.7 all-gather.5.cloned.1.call-update
  8.7 1.3 broadcast_in_dim.51
  9.9 11.1 %all-to-all-start.2 = ((s32[32,1,2]{2,1,0:T(1,128)}), s32[32,1,2]{2,1,0:T(1,128)S(1)}, u32[]{:S(2)}, u32[]{:S(2)}) async-start(s32[32,1,2]{2,1,0:T(1,128)} %broadcast_in_dim.51), calls=%async_computation.2 | async-start | bytes 32768 | tf_op jit(solution)/shard_map/all_to_all | solution.py:15
  21.1 0.8 copy.15
  21.9 0.1 reshape.94
  22.0 0.1 reshape.93
  22.1 0.9 gather_fusion
  23.0 5.9 %all-to-all-done.2 = s32[32,1,2]{2,1,0:T(1,128)S(1)} async-done(((s32[32,1,2]{2,1,0:T(1,128)}), s32[32,1,2]{2,1,0:T(1,128)S(1)}, u32[]{:S(2)}, u32[]{:S(2)}) %all-to-all-start.2) | async-done | bytes 288 | tf_op jit(solution)/shard_map/all_to_all | solution.py:15
  28.9 1.3 broadcast_in_dim.50
  30.1 4.3 %all-to-all-start.1 = ((s32[32,1,2]{2,1,0:T(1,128)}), s32[32,1,2]{2,1,0:T(1,128)S(1)}, u32[]{:S(2)}, u32[]{:S(2)}) async-start(s32[32,1,2]{2,1,0:T(1,128)} %broadcast_in_dim.50), calls=%async_computation.1 | async-start | bytes 32768 | tf_op jit(solution)/shard_map/all_to_all | solution.py:15
  34.4 0.1 broadcast_select_fusion.1
  34.5 0.1 copy.17
  34.6 7.6 %all-to-all-done.1 = s32[32,1,2]{2,1,0:T(1,128)S(1)} async-done(((s32[32,1,2]{2,1,0:T(1,128)}), s32[32,1,2]{2,1,0:T(1,128)S(1)}, u32[]{:S(2)}, u32[]{:S(2)}) %all-to-all-start.1) | async-done | bytes 288 | tf_op jit(solution)/shard_map/all_to_all | solution.py:15
  42.3 1.6 broadcast_in_dim.45
  43.8 4.5 %all-to-all-start = ((bf16[32,256,128]{1,2,0:T(8,128)(2,1)}), bf16[32,256,128]{1,2,0:T(8,128)(2,1)S(1)}, u32[]{:S(2)}, u32[]{:S(2)}) async-start(bf16[32,256,128]{1,2,0:T(8,128)(2,1)} %broadcast_in_dim.45), calls=%async_computation | async-start | bytes 4194304 | tf_op jit(solution)/shard_map/all_to_all | solution.py:15
  48.4 0.1 mul.47
  48.5 5.6 %gather_fusion.1 = bf16[256,1792]{1,0:T(8,128)(2,1)} fusion(bf16[1024,1792]{1,0:T(8,128)(2,1)} %param.10, s32[1024]{0:T(1024)S(1)} %pad_clamp_fusion), kind=kCustom, calls=%fused_computation.1 | custom fusion | bytes 1836032 | tf_op jit(solution)/shard_map/jit(_take)/gather | solution.py:46
  54.1 1.3 broadcast_select_fusion
  55.5 0.1 convert_element_type.28
  55.6 0.5 broadcast.138
  56.1 0.7 reduce.7
  56.8 0.1 lt.62
  56.9 0.2 convert_reduce_fusion
  57.2 0.1 mul.54
  57.3 1.9 fusion
  59.2 38.7 %all-to-all-done = bf16[32,256,128]{1,2,0:T(8,128)(2,1)S(1)} async-done(((bf16[32,256,128]{1,2,0:T(8,128)(2,1)}), bf16[32,256,128]{1,2,0:T(8,128)(2,1)S(1)}, u32[]{:S(2)}, u32[]{:S(2)}) %all-to-all-start) | async-done | bytes 2097184 | tf_op jit(solution)/shard_map/all_to_all | solution.py:15
  97.9 45.3 %all-gather.3.cloned.1.call-done = bf16[896,4096]{1,0:T(8,128)(2,1)} async-done(((bf16[896,512]{1,0:T(8,128)(2,1)}), bf16[896,4096]{1,0:T(8,128)(2,1)}) %all-gather.3.cloned.1.call-update) | async-done | bytes 7340048 | tf_op jit(solution)/shard_map/all_gather | solution.py:60
  143.3 5.6 %fusion.4 = f32[896,8]{0,1:T(8,128)S(1)} fusion(bf16[896,4096]{1,0:T(8,128)(2,1)} %all-gather.3.cloned.1.call-done, bf16[256,4096]{0,1:T(8,128)(2,1)S(1)} %bitcast.13, s32[]{:T(128)S(6)} %select_n.57, f32[8]{0:T(128)S(1)} %mul.47, s32[896]{0:T(1024)S(1)} %add_select_fusion, s32[8]{0:T(128)S(1)} %and_select_fusion), kind=kOutput, calls=%fused_computation.8 | convolution fusion | flops 58741760 | bytes 8422404 | tf_op jit(solution)/shard_map/dot_general | solution.py:62
  148.9 84.6 %all-gather.5.cloned.1.call-done = bf16[4096,1792]{1,0:T(8,128)(2,1)} async-done(((bf16[128,1792]{1,0:T(8,128)(2,1)}), bf16[4096,1792]{1,0:T(8,128)(2,1)}) %all-gather.5.cloned.1.call-update) | async-done | bytes 14680080 | tf_op jit(solution)/shard_map/all_gather | solution.py:59
  233.5 17.0 %fusion.15 = f32[896,1792]{1,0:T(8,128)S(1)} fusion(bf16[896,4096]{1,0:T(8,128)(2,1)} %all-gather.3.cloned.1.call-done, bf16[4096,1792]{1,0:T(8,128)(2,1)} %all-gather.5.cloned.1.call-done), kind=kOutput, calls=%fused_computation.38 | convolution fusion | flops 13153337344 | bytes 28442624 | tf_op jit(solution)/shard_map/dot_general | solution.py:61
  250.5 4.7 %add_convert_fusion = bf16[896,1792]{1,0:T(8,128)(2,1)} fusion(f32[896,1792]{1,0:T(8,128)S(1)} %fusion.15, f32[896,8]{0,1:T(8,128)S(1)} %fusion.4, bf16[256,1792]{1,0:T(8,128)(2,1)S(1)} %broadcast_select_fusion, s32[]{:T(128)S(6)} %select_n.57), kind=kOutput, calls=%fused_computation.2 | convolution fusion | flops 157351936 | bytes 9691140 | tf_op jit(solution)/shard_map/dot_general | solution.py:66
  (16 shorter events, 0.3 us)
Async XLA Ops:
  7.2 15.0 %copy-start = (bf16[1024,128]{1,0:T(8,128)(2,1)S(1)}, bf16[1024,128]{1,0:T(8,128)(2,1)}, u32[]{:S(2)}) copy-start(bf16[1024,128]{1,0:T(8,128)(2,1)} %param.9) | copy-start | bytes 786436
  7.2 41.1 %copy-start.1 = (s32[2]{0:T(128)S(1)}, s32[2]{0:T(128)}, u32[]{:S(2)}) copy-start(s32[2]{0:T(128)} %param.12) | copy-start | bytes 28
  7.2 136.1 %all-gather.3.cloned.1.call-start = ((), (), s32[]{:S(2)}) async-start(), calls=%async_computation.3 | async-start | bytes 8257536 | tf_op jit(solution)/shard_map/all_gather | solution.py:60
  7.9 225.6 %all-gather.5.cloned.1.call-start = ((), (), s32[]{:S(2)}) async-start(), calls=%async_computation.4 | async-start | bytes 15138816 | tf_op jit(solution)/shard_map/all_gather | solution.py:59
  9.9 18.9 %all-to-all-start.2 = ((s32[32,1,2]{2,1,0:T(1,128)}), s32[32,1,2]{2,1,0:T(1,128)S(1)}, u32[]{:S(2)}, u32[]{:S(2)}) async-start(s32[32,1,2]{2,1,0:T(1,128)} %broadcast_in_dim.51), calls=%async_computation.2 | async-start | bytes 32768 | tf_op jit(solution)/shard_map/all_to_all | solution.py:15
  30.1 12.2 %all-to-all-start.1 = ((s32[32,1,2]{2,1,0:T(1,128)}), s32[32,1,2]{2,1,0:T(1,128)S(1)}, u32[]{:S(2)}, u32[]{:S(2)}) async-start(s32[32,1,2]{2,1,0:T(1,128)} %broadcast_in_dim.50), calls=%async_computation.1 | async-start | bytes 32768 | tf_op jit(solution)/shard_map/all_to_all | solution.py:15
  43.8 54.1 %all-to-all-start = ((bf16[32,256,128]{1,2,0:T(8,128)(2,1)}), bf16[32,256,128]{1,2,0:T(8,128)(2,1)S(1)}, u32[]{:S(2)}, u32[]{:S(2)}) async-start(bf16[32,256,128]{1,2,0:T(8,128)(2,1)} %broadcast_in_dim.45), calls=%async_computation | async-start | bytes 4194304 | tf_op jit(solution)/shard_map/all_to_all | solution.py:15
Sparse Core Ops, SparseCore 0:
  10.5 132.7 all-gather.2
  145.1 88.3 all-gather.4
where the time goes:
time: 262 us
  waiting for transfers between devices  184 us (70%)
  matrix products  29.2 us (11%)
  starting transfers between devices  20 us (8%)
  between operations  14.2 us (5%)
  local copies, waits for them, and re-layouts  12.7 us (5%)
    all_gather x1, waiting for transfers between devices, per_device(): entire_weight = lax.all_gather(up_weight, 'pop', axis=0, tiled=True)  84.6 us
    all_to_all x3, waiting for transfers between devices, sent_to_all(): return lax.all_to_all(copies, axis, split_axis=0, concat_axis=0, tiled=True)  52.3 us
    all_gather x1, waiting for transfers between devices, per_device(): piece = lax.all_gather(tokens, 'fsdp', axis=1, tiled=True)  45.3 us
    all_to_all x3, starting transfers between devices, sent_to_all(): return lax.all_to_all(copies, axis, split_axis=0, concat_axis=0, tiled=True)  19.9 us
    dot_general x1, matrix products, per_device(): jnp.dot(piece, entire_weight, preferred_element_type=jnp.float32)  17 us
    dot_general x1, matrix products, per_device(): low_sum = jnp.dot(piece, own_a.T, preferred_element_type=jnp.float32)  5.63 us
    gather x1, local copies, waits for them, and re-layouts, per_device(): picked_b = jnp.take(b_bank, flat_index, axis=0)  5.58 us
  transfers between devices with their start and end apart: 5, of which 5 were waited for; matrix products, arithmetic and copies ran while one was open for 9% of the time, Pallas kernels for 0%

commit v1 on v0

--- a/solution.py
+++ b/solution.py
@@ -1,3 +1,4 @@
+import functools
 import math
 import jax
 import jax.numpy as jnp
@@ -8,6 +9,18 @@
 RANK = 4
 SEQ = 448
 noise_scale = 0.5
+
+
+def _turn_node(m, mesh_ax):
+    return jnp.concatenate(
+        lax.all_to_all(
+            jnp.stack([m for _ in range(lax.axis_size(mesh_ax))], axis=0), mesh_ax, 0, 0
+        ),
+        axis=0,
+    )
+
+
+scales_feed = functools.partial(_turn_node, mesh_ax="pop")
 
 
 def sent_to_all(array, axis):
@@ -56,7 +69,7 @@
     column_factor = jnp.repeat(noise_scale / math.sqrt(D * RANK) * own_signs, RANK)
     member_of_column = jnp.arange(own_width) // RANK
     row_count = tokens.shape[0]
-    entire_weight = lax.all_gather(up_weight, "pop", axis=0, tiled=True)
+    entire_weight = scales_feed(up_weight)
     piece = lax.all_gather(tokens, "fsdp", axis=1, tiled=True)
     dense_sum = jnp.dot(piece, entire_weight, preferred_element_type=jnp.float32)
     low_sum = jnp.dot(piece, own_a.T, preferred_element_type=jnp.float32)

time: 262 us -> 460 us (1.76); the launches traced: 262 us -> 452 us
  waiting for transfers between devices: 184 us -> 314 us
  blocking collectives: 0 us -> 52.4 us
  local copies, waits for them, and re-layouts: 12.7 us -> 18.3 us
    all_to_all x0 -> x1, waiting for transfers between devices: none -> 139 us  [_turn_node(): lax.all_to_all(jnp.stack([m for _ in range(lax.axis_size(mesh_ax))], axis...]
    all_gather x1, waiting for transfers between devices: 45.3 us -> 160 us  [per_device(): piece = lax.all_gather(tokens, 'fsdp', axis=1, tiled=True)]
    all_gather x1 -> x0, waiting for transfers between devices: 84.6 us -> none  [per_device(): entire_weight = lax.all_gather(up_weight, 'pop', axis=0, tiled=True)]
    all_to_all x0 -> x1, blocking collectives: none -> 52.4 us  [sent_to_all(): return lax.all_to_all(copies, axis, split_axis=0, concat_axis=0, tiled=True)]
    all_to_all x3 -> x2, waiting for transfers between devices: 52.3 us -> 13.5 us  [sent_to_all(): return lax.all_to_all(copies, axis, split_axis=0, concat_axis=0, tiled=True)]
    all_to_all x0 -> x1, starting transfers between devices: none -> 7.05 us  [_turn_node(): lax.all_to_all(jnp.stack([m for _ in range(lax.axis_size(mesh_ax))], axis...]
    another operation x0 -> x1, local copies, waits for them, and re-layouts: none -> 6.84 us  [_turn_node(): jnp.stack([m for _ in range(lax.axis_size(mesh_ax))], axis=0)]
    all_to_all x3 -> x2, starting transfers between devices: 19.9 us -> 15.4 us  [sent_to_all(): return lax.all_to_all(copies, axis, split_axis=0, concat_axis=0, tiled=True)]
  transfers between devices with their start and end apart: 5 -> 4, of which waited for: 5 -> 4; matrix products, arithmetic and copies ran while one was open for 9% -> 4% of each run, Pallas kernels for 0% -> 0%
where the time goes in v1:
time: 460 us; the launch traced here: 452 us
  waiting for transfers between devices  314 us (68%)
  blocking collectives  52.4 us (11%)
  matrix products  28.7 us (6%)
  starting transfers between devices  22.7 us (5%)
  local copies, waits for them, and re-layouts  18.3 us (4%)
  between operations  14.2 us (3%)
    all_gather x1, waiting for transfers between devices, per_device(): piece = lax.all_gather(tokens, 'fsdp', axis=1, tiled=True)  160 us
    all_to_all x1, waiting for transfers between devices, _turn_node(): lax.all_to_all(jnp.stack([m for _ in range(lax.axis_size(mesh_ax))], axis...  139 us
    all_to_all x1, blocking collectives, sent_to_all(): return lax.all_to_all(copies, axis, split_axis=0, concat_axis=0, tiled=True)  52.4 us
    dot_general x1, matrix products, per_device(): jnp.dot(piece, entire_weight, preferred_element_type=jnp.float32)  16.7 us
    all_to_all x2, starting transfers between devices, sent_to_all(): return lax.all_to_all(copies, axis, split_axis=0, concat_axis=0, tiled=True)  15.4 us
    all_to_all x2, waiting for transfers between devices, sent_to_all(): return lax.all_to_all(copies, axis, split_axis=0, concat_axis=0, tiled=True)  13.5 us
  transfers between devices with their start and end apart: 4, of which 4 were waited for; matrix products, arithmetic and copies ran while one was open for 4% of the time, Pallas kernels for 0%

profile of v1, /device:TPU:1, one launch (start us, length us, event | category | flops | bytes accessed | tf_op | source)
XLA Modules:
  0.0 452.4 jit_solution(1466194191540169315)
XLA Ops:
  7.2 1.3 broadcast_in_dim.51
  8.5 11.1 %all-to-all-start.3 = ((s32[32,1,2]{2,1,0:T(1,128)}), s32[32,1,2]{2,1,0:T(1,128)S(1)}, u32[]{:S(2)}, u32[]{:S(2)}) async-start(s32[32,1,2]{2,1,0:T(1,128)} %broadcast_in_dim.51), calls=%async_computation.3 | async-start | bytes 32768 | tf_op jit(solution)/shard_map/all_to_all | solution.py:28
  19.7 0.8 copy.15
  20.4 0.1 reshape.100
  20.5 0.1 reshape.99
  20.7 0.9 gather_fusion
  21.6 5.9 %all-to-all-done.3 = s32[32,1,2]{2,1,0:T(1,128)S(1)} async-done(((s32[32,1,2]{2,1,0:T(1,128)}), s32[32,1,2]{2,1,0:T(1,128)S(1)}, u32[]{:S(2)}, u32[]{:S(2)}) %all-to-all-start.3) | async-done | bytes 288 | tf_op jit(solution)/shard_map/all_to_all | solution.py:28
  27.4 1.3 broadcast_in_dim.50
  28.7 4.3 all-to-all-start.2
  33.0 0.1 broadcast_select_fusion.1
  33.1 0.1 copy.17
  33.2 7.6 %all-to-all-done.2 = s32[32,1,2]{2,1,0:T(1,128)S(1)} async-done(((s32[32,1,2]{2,1,0:T(1,128)}), s32[32,1,2]{2,1,0:T(1,128)S(1)}, u32[]{:S(2)}, u32[]{:S(2)}) %all-to-all-start.2) | async-done | bytes 288 | tf_op jit(solution)/shard_map/all_to_all | solution.py:28
  40.9 0.2 broadcast_in_dim.45
  41.1 52.4 %all_to_all.22 = bf16[32,256,128]{1,2,0:T(8,128)(2,1)S(1)} all-to-all(bf16[32,256,128]{1,2,0:T(8,128)(2,1)S(1)} %broadcast_in_dim.45), channel_id=1, replica_groups=mesh['pop'=32,'fsdp'=8] {'pop'}, dimensions={0} | all-to-all | bytes 4194304 | tf_op jit(solution)/shard_map/all_to_all | solution.py:28
  93.5 6.8 %stack.2 = bf16[32,128,1792]{2,1,0:T(8,128)(2,1)} broadcast(bf16[128,1792]{1,0:T(8,128)(2,1)S(1)} %copy-done.1), dimensions={1,2} | broadcast | bytes 15138816 | tf_op jit(solution)/shard_map/stack | solution.py:17
  100.4 7.1 %all-to-all-start = ((bf16[32,128,1792]{2,1,0:T(8,128)(2,1)}), bf16[32,128,1792]{2,1,0:T(8,128)(2,1)}, u32[]{:S(2)}, u32[]{:S(2)}) async-start(bf16[32,128,1792]{2,1,0:T(8,128)(2,1)} %stack.2), calls=%async_computation | async-start | bytes 29360128 | tf_op jit(solution)/shard_map/all_to_all | solution.py:16
  107.4 0.2 all-gather.2.cloned.1.call-start
  107.6 0.5 all-gather.2.cloned.1.call-update
  108.3 5.6 %gather_fusion.1 = bf16[256,1792]{1,0:T(8,128)(2,1)} fusion(bf16[1024,1792]{1,0:T(8,128)(2,1)} %param.10, s32[1024]{0:T(1024)S(1)} %pad_clamp_fusion), kind=kCustom, calls=%fused_computation.1 | custom fusion | bytes 1836032 | tf_op jit(solution)/shard_map/jit(_take)/gather | solution.py:59
  113.9 1.3 broadcast_select_fusion
  115.3 0.1 convert_element_type.28
  115.4 0.5 broadcast.140
  116.0 0.7 reduce.7
  116.7 0.1 lt.62
  116.8 0.2 convert_reduce_fusion
  117.0 0.1 mul.54
  117.1 1.9 fusion
  119.0 160.4 %all-gather.2.cloned.1.call-done = bf16[896,4096]{1,0:T(8,128)(2,1)} async-done(((bf16[896,512]{1,0:T(8,128)(2,1)}), bf16[896,4096]{1,0:T(8,128)(2,1)}) %all-gather.2.cloned.1.call-update) | async-done | bytes 7340048 | tf_op jit(solution)/shard_map/all_gather | solution.py:73
  279.4 5.6 %fusion.4 = f32[896,8]{0,1:T(8,128)S(1)} fusion(bf16[896,4096]{1,0:T(8,128)(2,1)} %all-gather.2.cloned.1.call-done, bf16[256,4096]{0,1:T(8,128)(2,1)S(1)} %bitcast.14, s32[]{:T(128)S(6)} %select_n.57, f32[8]{0:T(128)S(1)} %mul.47, s32[896]{0:T(1024)S(1)} %add_select_fusion, s32[8]{0:T(128)S(1)} %and_select_fusion), kind=kOutput, calls=%fused_computation.8 | convolution fusion | flops 58741760 | bytes 8422404 | tf_op jit(solution)/shard_map/dot_general | solution.py:75
  285.0 139.4 %all-to-all-done = bf16[32,128,1792]{2,1,0:T(8,128)(2,1)} async-done(((bf16[32,128,1792]{2,1,0:T(8,128)(2,1)}), bf16[32,128,1792]{2,1,0:T(8,128)(2,1)}, u32[]{:S(2)}, u32[]{:S(2)}) %all-to-all-start) | async-done | bytes 14680096 | tf_op jit(solution)/shard_map/all_to_all | solution.py:16
  424.4 16.7 %fusion.15 = f32[896,1792]{1,0:T(8,128)S(1)} fusion(bf16[896,4096]{1,0:T(8,128)(2,1)} %all-gather.2.cloned.1.call-done, bf16[4096,1792]{1,0:T(8,128)(2,1)} %bitcast), kind=kOutput, calls=%fused_computation.38 | convolution fusion | flops 13153337344 | bytes 28442624 | tf_op jit(solution)/shard_map/dot_general | solution.py:74
  441.1 4.4 add_convert_fusion
  (17 shorter events, 0.3 us)
Async XLA Ops:
  7.2 13.5 %copy-start = (bf16[1024,128]{1,0:T(8,128)(2,1)S(1)}, bf16[1024,128]{1,0:T(8,128)(2,1)}, u32[]{:S(2)}) copy-start(bf16[1024,128]{1,0:T(8,128)(2,1)} %param.9) | copy-start | bytes 786436
  7.2 86.3 %copy-start.1 = (bf16[128,1792]{1,0:T(8,128)(2,1)S(1)}, bf16[128,1792]{1,0:T(8,128)(2,1)}, u32[]{:S(2)}) copy-start(bf16[128,1792]{1,0:T(8,128)(2,1)} %param.8) | copy-start | bytes 1376260
  8.5 18.9 %all-to-all-start.3 = ((s32[32,1,2]{2,1,0:T(1,128)}), s32[32,1,2]{2,1,0:T(1,128)S(1)}, u32[]{:S(2)}, u32[]{:S(2)}) async-start(s32[32,1,2]{2,1,0:T(1,128)} %broadcast_in_dim.51), calls=%async_computation.3 | async-start | bytes 32768 | tf_op jit(solution)/shard_map/all_to_all | solution.py:28
  28.7 12.1 %all-to-all-start.2 = ((s32[32,1,2]{2,1,0:T(1,128)}), s32[32,1,2]{2,1,0:T(1,128)S(1)}, u32[]{:S(2)}, u32[]{:S(2)}) async-start(s32[32,1,2]{2,1,0:T(1,128)} %broadcast_in_dim.50), calls=%async_computation.2 | async-start | bytes 32768 | tf_op jit(solution)/shard_map/all_to_all | solution.py:28
  100.4 7.8 %copy-start.2 = (s32[2]{0:T(128)S(1)}, s32[2]{0:T(128)}, u32[]{:S(2)}) copy-start(s32[2]{0:T(128)} %param.12) | copy-start | bytes 28
  100.4 324.0 %all-to-all-start = ((bf16[32,128,1792]{2,1,0:T(8,128)(2,1)}), bf16[32,128,1792]{2,1,0:T(8,128)(2,1)}, u32[]{:S(2)}, u32[]{:S(2)}) async-start(bf16[32,128,1792]{2,1,0:T(8,128)(2,1)} %stack.2), calls=%async_computation | async-start | bytes 29360128 | tf_op jit(solution)/shard_map/all_to_all | solution.py:16
  107.4 172.0 %all-gather.2.cloned.1.call-start = ((), (), s32[]{:S(2)}) async-start(), calls=%async_computation.4 | async-start | bytes 8257536 | tf_op jit(solution)/shard_map/all_gather | solution.py:73
Sparse Core Ops, SparseCore 0:
  110.7 168.6 all-gather.1
